TPU v7x, 256 devices: a whole 4x4x8 slice. The times are simulated.
256 devices in a mesh: ctx: 64 (over z_lo, x, y), tp: 4 (over z_hi, core).
Axes of the slice: x: 4, y: 4, z: 8 (z_hi: 2, z_lo: 4; z = z_hi * 4 + z_lo), core: 2. Of those that a mesh axis runs over, the one named last changes fastest.
Arguments:
- step_inputs: bfloat16 [8192, 8192], P('ctx', 'tp'), may hold values from -6 to 6
- log_decay: float32 [8192, 128], P('ctx', 'tp'), may hold values from -0.7 to 0
- write_vecs: bfloat16 [8192, 2048], P('ctx', 'tp'), may hold values from -6 to 6
- read_vecs: bfloat16 [8192, 2048], P('ctx', 'tp'), may hold values from -0.375 to 0.375
- gate_vals: bfloat16 [8192, 8192], P('ctx', 'tp'), may hold values from -6 to 6
- skip_gain: float32 [128], P('tp'), may hold values from 0.5 to 2
- norm_gain: float32 [8192], P('tp'), may hold values from 0.5 to 1.5
- query_rows: bfloat16 [8192, 4096], P('ctx', 'tp'), may hold values from -160 to 160
- key_rows: bfloat16 [8192, 1024], P('ctx', 'tp'), may hold values from -6 to 6
- value_rows: bfloat16 [8192, 1024], P('ctx', 'tp'), may hold values from -6 to 6
Outputs:
- mamba_out: bfloat16 [8192, 8192], P('ctx', 'tp')
- attn_out: bfloat16 [8192, 4096], P('ctx', 'tp')
All inputs are finite; a program needn't handle non-finite values.
Results may differ from a plain program's by a relative error of at most 0.0049.
Values may be sent and summed in bfloat16 or wider, within the bound.
No kernel may reach another device: no remote copies, remote signals or barrier semaphores. Data moves between devices by JAX's collectives and lax.ppermute only.
A program may use at most 320 MiB of HBM per device.

v0:
```python
import jax
import jax.numpy as jnp
from jax import lax
from jax.sharding import PartitionSpec as P

MHDIM = 64
NSTATE = 256
HDIM = 128


eps_norm = 1e-05
neg_large = -1e30
block_span = 2048


def entering_2(part, axis, combine, identity):
    place = lax.axis_index(axis)
    gathered = jax.tree.map(lambda a: lax.all_gather(a, axis), part)
    state = jax.tree.map(lambda a, e: jnp.zeros_like(a) + jnp.asarray(e, a.dtype), part, identity)

    def one(turn, state):
        return combine(
            state, jax.tree.map(lambda a: lax.dynamic_index_in_dim(a, turn, 0, False), gathered)
        )

    return lax.fori_loop(0, place, one, state)


def attend_half(half_state, queries, query_pos, key_block, value_block, key_pos):
    run_max, run_sum, accumulated = half_state
    scores = jnp.einsum(
        "qkgd,nkd->qkgn", queries, key_block, preferred_element_type=jnp.float32
    ) * HDIM ** (-0.5)
    allowed = (key_pos[None, :] <= query_pos[:, None])[:, None, None, :]
    scores = jnp.where(allowed, scores, neg_large)
    new_max = jnp.maximum(run_max, jnp.max(scores, axis=3))
    expo_weights = jnp.where(allowed, jnp.exp(scores - new_max[..., None]), 0.0)
    factor = jnp.exp(run_max - new_max)
    run_sum = run_sum * factor + jnp.sum(expo_weights, axis=3)
    summed = jnp.einsum(
        "qkgn,nkd->qkgd",
        expo_weights.astype(jnp.bfloat16),
        value_block,
        preferred_element_type=jnp.float32,
    )
    accumulated = accumulated * factor[..., None] + summed
    return (new_max, run_sum, accumulated)


def on_device(
    step_inputs,
    log_decay,
    write_vecs,
    read_vecs,
    gate_vals,
    skip_gain,
    norm_gain,
    query_rows,
    key_rows,
    value_rows,
):
    length = step_inputs.shape[0]
    heads = log_decay.shape[1]
    groups = write_vecs.shape[1] // NSTATE
    per_group = heads // groups
    inputs_grid = step_inputs.reshape(length, groups, per_group, MHDIM)
    write_grid = write_vecs.reshape(length, groups, NSTATE)
    read_grid = read_vecs.reshape(length, groups, NSTATE)
    cumulative = jnp.cumsum(log_decay, axis=0)
    last_cum = cumulative[length - 1]
    positions = jnp.arange(length, dtype=jnp.int32)
    causal_mask = positions[:, None] >= positions[None, :]
    pair_dots = jnp.einsum(
        "tgn,sgn->gts", read_grid, write_grid, preferred_element_type=jnp.float32
    )
    cum_gaps = cumulative.T[:, :, None] - cumulative.T[:, None, :]
    decays = jnp.where(causal_mask[None], jnp.exp(jnp.where(causal_mask[None], cum_gaps, 0.0)), 0.0)
    weights = (decays.reshape(groups, per_group, length, length) * pair_dots[:, None]).astype(
        jnp.bfloat16
    )
    local_out = jnp.einsum(
        "ghts,sghp->tghp", weights, inputs_grid, preferred_element_type=jnp.float32
    )
    tail_decay = jnp.exp(last_cum[None, :] - cumulative).reshape(length, groups, per_group, 1)
    decayed = (inputs_grid * tail_decay).astype(jnp.bfloat16)
    block_state = jnp.einsum(
        "sghp,sgn->ghpn", decayed, write_grid, preferred_element_type=jnp.float32
    )
    block_state = block_state.reshape(heads, MHDIM, NSTATE)

    def combine(earlier, latter):
        return (earlier[0] * latter[0], latter[0][:, None, None] * earlier[1] + latter[1])

    identity = (jnp.ones((heads,), jnp.float32), jnp.zeros((heads, MHDIM, NSTATE), jnp.float32))
    entering = entering_2((jnp.exp(last_cum), block_state), "ctx", combine, identity)
    carried_grid = entering[1].reshape(groups, per_group, MHDIM, NSTATE)
    inflow = jnp.einsum(
        "tgn,ghpn->tghp",
        read_grid.astype(jnp.float32),
        carried_grid,
        precision=lax.Precision.HIGHEST,
    )
    inflow = inflow * jnp.exp(cumulative).reshape(length, groups, per_group, 1)
    mixed_out = local_out + inflow + skip_gain.reshape(groups, per_group, 1) * inputs_grid
    gated_vals = mixed_out.reshape(length, heads * MHDIM) * jax.nn.silu(
        gate_vals.astype(jnp.float32)
    )
    group_vals = gated_vals.reshape(length, groups, per_group * MHDIM)
    squares = jnp.mean(group_vals * group_vals, axis=2, keepdims=True)
    normed = (group_vals * lax.rsqrt(squares + eps_norm)).reshape(length, heads * MHDIM)
    mamba_out = (normed * norm_gain).astype(jnp.bfloat16)
    kv_local = key_rows.shape[1] // HDIM
    q_local = query_rows.shape[1] // HDIM
    group_share = q_local // kv_local
    half_rows = length // 2
    ctx_index = lax.axis_index("ctx")
    first_pos = ctx_index * length + jnp.arange(half_rows, dtype=jnp.int32)
    second_pos = ctx_index * length + half_rows + jnp.arange(half_rows, dtype=jnp.int32)
    query_pos = jnp.stack([first_pos, second_pos])
    last_pos = jnp.max(query_pos, axis=1)
    work_grid = query_rows.reshape(2, half_rows, kv_local, group_share, HDIM)

    def attend_block(carried_state, key_block, value_block, key_start):
        key_pos = key_start + jnp.arange(key_block.shape[0], dtype=jnp.int32)
        updated = []
        for half_index in range(2):
            half_state = (
                carried_state[0][half_index],
                carried_state[1][half_index],
                carried_state[2][half_index],
            )

            def apply_block(held, half_index=half_index):
                return attend_half(
                    held,
                    work_grid[half_index],
                    query_pos[half_index],
                    key_block,
                    value_block,
                    key_pos,
                )

            def keep_block(held):
                return held

            updated.append(
                lax.cond(key_start <= last_pos[half_index], apply_block, keep_block, half_state)
            )
        return tuple((jnp.stack([updated[0][member], updated[1][member]]) for member in range(3)))

    start_state = (
        jnp.full((2, half_rows, kv_local, group_share), neg_large, jnp.float32),
        jnp.zeros((2, half_rows, kv_local, group_share), jnp.float32),
        jnp.zeros((2, half_rows, kv_local, group_share, HDIM), jnp.float32),
    )
    pieces = (
        lax.all_gather(key_rows, "ctx", axis=0, tiled=True),
        lax.all_gather(value_rows, "ctx", axis=0, tiled=True),
    )
    piece_rows = pieces[0].shape[0]
    key_grid = pieces[0].reshape(piece_rows, kv_local, HDIM)
    value_grid = pieces[1].reshape(piece_rows, kv_local, HDIM)

    def step_fn(inner_state, block_index):
        offset = block_index * block_span
        key_block = lax.dynamic_slice_in_dim(key_grid, offset, block_span, 0)
        value_block = lax.dynamic_slice_in_dim(value_grid, offset, block_span, 0)
        return (attend_block(inner_state, key_block, value_block, offset), None)

    result, _ = lax.scan(
        step_fn, start_state, jnp.arange(piece_rows // block_span, dtype=jnp.int32)
    )
    final_state = result
    result = final_state[2] / final_state[1][..., None]
    result = result.reshape(length, q_local * HDIM).astype(jnp.bfloat16)
    return (mamba_out, result)


def solution(mesh):
    in_specs = (
        P("ctx", "tp"),
        P("ctx", "tp"),
        P("ctx", "tp"),
        P("ctx", "tp"),
        P("ctx", "tp"),
        P("tp"),
        P("tp"),
        P("ctx", "tp"),
        P("ctx", "tp"),
        P("ctx", "tp"),
    )
    out_specs = (P("ctx", "tp"), P("ctx", "tp"))
    return jax.shard_map(
        on_device, mesh=mesh, in_specs=in_specs, out_specs=out_specs, check_vma=False
    )
```

profile of v0, /device:TPU:254, one launch (start us, length us, event | category | flops | bytes accessed | tf_op | source)
XLA Modules:
  0.0 2194.5 jit_solution(17525775318747400105)
XLA Ops:
  18.3 182.0 %all-gather = f32[64,1,32]{2,1,0:T(1,128)} all-gather(f32[1,1,32]{2,1,0:T(1,128)S(1)} %get-tuple-element.368), channel_id=1, replica_groups=mesh['ctx'=64,'tp'=4] {'ctx'}, dimensions={0}, use_global_device_ids=true | all-gather | bytes 8320 | tf_op jit(solution)/shard_map/all_gather | solution.py:18
  202.5 87.4 %all-gather.7.cloned.1.call-done = bf16[8192,256]{0,1:T(8,128)(2,1)} async-done(((bf16[128,256]{0,1:T(8,128)(2,1)}), bf16[8192,256]{0,1:T(8,128)(2,1)}) %all-gather.7.cloned.1.call-update) | async-done | bytes 4194320 | tf_op jit(solution)/shard_map/all_gather | solution.py:157
  289.9 280.6 %all-gather.9.cloned.1.call-done = bf16[8192,256]{0,1:T(8,128)(2,1)} async-done(((bf16[128,256]{0,1:T(8,128)(2,1)}), bf16[8192,256]{0,1:T(8,128)(2,1)}) %all-gather.9.cloned.1.call-update) | async-done | bytes 4194320 | tf_op jit(solution)/shard_map/all_gather | solution.py:158
  571.9 100.2 %while.28 = (s32[]{:T(128)}, f32[2,64,2,4]{1,3,2,0:T(4,128)S(1)}, f32[2,64,2,4]{1,3,2,0:T(4,128)S(1)}, f32[2,64,2,4,128]{4,1,3,2,0:T(8,128)}, s32[4]{0:T(128)}, ...) while((s32[]{:T(128)}, f32[2,64,2,4]{1,3,2,0:T(4,128)S(1)}, ...), condition=%wide.region_14.15_spmd.clone, body=%wide.region_5.14_spmd.clone.sunk | while | flops 1101666432 | bytes 42330608 | solution.py:170
  581.0 6.6 conditional.7
  585.4 2.2 fusion.16
  588.8 6.5 conditional.6
  593.2 2.2 fusion.39
  606.1 6.6 conditional.7
  610.5 2.2 fusion.16
  613.9 6.5 conditional.6
  618.3 2.2 fusion.39
  631.2 6.6 conditional.7
  635.5 2.2 fusion.16
  639.0 6.5 conditional.6
  643.3 2.2 fusion.39
  656.2 6.6 conditional.7
  660.6 2.2 fusion.16
  664.0 6.5 conditional.6
  668.4 2.2 fusion.39
  674.4 1330.4 %all-gather.5.cloned.1.call-done = f32[64,32,64,256]{3,2,1,0:T(8,128)} async-done(((f32[1,32,64,256]{3,2,1,0:T(8,128)}), f32[64,32,64,256]{3,2,1,0:T(8,128)}) %all-gather.5.cloned.1.call-update) | async-done | bytes 134217744 | tf_op jit(solution)/shard_map/all_gather | solution.py:18
  2005.1 173.4 %while.27 = (s32[]{:T(128)}, f32[32,64,256]{2,1,0:T(8,128)S(1)}, s32[]{:T(128)}, f32[64,32]{1,0:T(8,128)}, f32[64,32,64,256]{3,2,1,0:T(8,128)}, /*index=5*/s32[]{:T(128)}, s32[]{:T(128)}, s32[]{:T(128)}) while((s32[]{:T(128)}, f32[32,64,256]{2,1,0:T(8,128)S(1)}, s32[]{:T(128)}, f32[64,32]{1,0:T(8,128)}, f32[64,32,64,256]{3,2,1,0:T(8,128)}, ...), condition=%wide.region_2.3_spmd, body=%wide.region_1.2_spmd.sunk | while | flops 1048581 | bytes 6291967 | solution.py:26
  2005.8 2.0 bitcast_add_fusion.2
  2008.6 2.0 bitcast_add_fusion.2
  2011.3 2.0 bitcast_add_fusion.2
  2014.1 2.0 bitcast_add_fusion.2
  2016.8 2.0 bitcast_add_fusion.2
  2019.6 2.0 bitcast_add_fusion.2
  2022.3 2.0 bitcast_add_fusion.2
  2025.1 2.0 bitcast_add_fusion.2
  2027.8 2.0 bitcast_add_fusion.2
  2030.6 2.0 bitcast_add_fusion.2
  2033.3 2.0 bitcast_add_fusion.2
  2036.1 2.0 bitcast_add_fusion.2
  2038.8 2.0 bitcast_add_fusion.2
  2041.6 2.0 bitcast_add_fusion.2
  2044.3 2.0 bitcast_add_fusion.2
  2047.1 2.0 bitcast_add_fusion.2
  2049.8 2.0 bitcast_add_fusion.2
  2052.6 2.0 bitcast_add_fusion.2
  2055.3 2.0 bitcast_add_fusion.2
  2058.0 2.0 bitcast_add_fusion.2
  2060.8 2.0 bitcast_add_fusion.2
  2063.5 2.0 bitcast_add_fusion.2
  2066.3 2.0 bitcast_add_fusion.2
  2069.0 2.0 bitcast_add_fusion.2
  2071.8 2.0 bitcast_add_fusion.2
  2178.5 3.3 fusion.52
  (272 shorter events, 218.3 us)
Async XLA Ops:
  7.2 193.2 %copy-start.3 = (bf16[128,512]{1,0:T(8,128)(2,1)S(1)}, bf16[128,512]{1,0:T(8,128)(2,1)}, u32[]{:S(2)}) copy-start(bf16[128,512]{1,0:T(8,128)(2,1)} %param.20) | copy-start | bytes 393220
  7.2 9.5 copy-start.4
  7.2 9.6 copy-start.9
  7.2 10.2 copy-start.5
  7.2 282.7 %all-gather.7.cloned.1.call-start = ((), (), s32[]{:S(2)}) async-start(), calls=%async_computation.1 | async-start | bytes 4259840 | tf_op jit(solution)/shard_map/all_gather | solution.py:157
  8.9 561.6 %all-gather.9.cloned.1.call-start = ((), (), s32[]{:S(2)}) async-start(), calls=%async_computation.2 | async-start | bytes 4259840 | tf_op jit(solution)/shard_map/all_gather | solution.py:158
  10.6 1994.2 %all-gather.5.cloned.1.call-start = ((), (), s32[]{:S(2)}) async-start(), calls=%async_computation | async-start | bytes 136314880 | tf_op jit(solution)/shard_map/all_gather | solution.py:18
  13.1 189.3 %copy-start = (bf16[128,2048]{0,1:T(8,128)(2,1)}, bf16[128,2048]{0,1:T(8,128)(2,1)S(1)}, u32[]{:S(2)}) copy-start(bf16[128,2048]{0,1:T(8,128)(2,1)S(1)} %copy.85) | copy-start | bytes 1572868
  2005.1 173.4 %copy-start.1 = (bf16[128,2048]{0,1:T(8,128)(2,1)S(1)}, bf16[128,2048]{0,1:T(8,128)(2,1)}, u32[]{:S(2)}) copy-start(bf16[128,2048]{0,1:T(8,128)(2,1)} %copy-done) | copy-start | bytes 1572868
  2005.1 173.4 %copy-start.6 = (f32[128,2,16]{0,2,1:T(8,128)S(1)}, f32[128,2,16]{0,2,1:T(8,128)}, u32[]{:S(2)}) copy-start(f32[128,2,16]{0,2,1:T(8,128)} %get-tuple-element.369) | copy-start | bytes 49156
  2005.1 173.4 %copy-start.8 = (f32[2,16]{1,0:T(2,128)S(1)}, f32[2,16]{1,0:T(2,128)}, u32[]{:S(2)}) copy-start(f32[2,16]{1,0:T(2,128)} %mul.131) | copy-start | bytes 388
  2183.4 3.3 copy-start.7
  2185.7 1.1 copy-start.2
Sparse Core Ops, SparseCore 0:
  10.3 279.5 all-gather.6
  291.6 278.8 all-gather.8
  572.3 1432.4 all-gather.4
where the time goes:
time: 2200 us; the launch traced here: 2190 us
  waiting for transfers between devices  1700 us (77%)
  blocking collectives  182 us (8%)
  other arithmetic  167 us (8%)
  local copies, waits for them, and re-layouts  90.6 us (4%)
  matrix products  31.9 us (1%)
    all_gather x1, waiting for transfers between devices, entering_2(): gathered = jax.tree.map(lambda a: lax.all_gather(a, axis), part)  1330 us
    all_gather x1, waiting for transfers between devices, on_device(): lax.all_gather(value_rows, 'ctx', axis=0, tiled=True)  281 us
    all_gather x1, blocking collectives, entering_2(): gathered = jax.tree.map(lambda a: lax.all_gather(a, axis), part)  182 us
    add x63, other arithmetic, combine(): latter[0][:, None, None] * earlier[1] + latter[1]  128 us
    all_gather x1, waiting for transfers between devices, on_device(): lax.all_gather(key_rows, 'ctx', axis=0, tiled=True)  87.4 us
  transfers between devices with their start and end apart: 3, of which 3 were waited for; matrix products, arithmetic and copies ran while one was open for 5% of the time, Pallas kernels for 0%

commit v1 on v0

v1 whole, which is shorter than its diff:
```python
import functools

import jax
import jax.numpy as jnp
from jax import lax
from jax.experimental import pallas as pl
from jax.experimental.pallas import tpu as pltpu
from jax.sharding import PartitionSpec as P

MHDIM = 64
NSTATE = 256
HDIM = 128
LBLK = 128
SLICE = 512
KVW = 2 * HDIM
TILE = 256

eps_norm = 1e-05
neg_large = -1e30
score_scale = HDIM ** (-0.5) * 1.4426950408889634

bf16 = jnp.bfloat16
f32 = jnp.float32
HIGHEST = lax.Precision.HIGHEST


def shape(dims, dtype):
    return jax.ShapeDtypeStruct(dims, dtype)


def run(kernel, outs, args, scratch=(), flops=1000000, moved=1000000):
    vmem = pl.BlockSpec(memory_space=pltpu.VMEM)
    smem = pl.BlockSpec(memory_space=pltpu.SMEM)
    return pl.pallas_call(
        kernel,
        out_shape=outs,
        in_specs=[smem] + [vmem] * (len(args) - 1),
        out_specs=[vmem] * len(outs),
        scratch_shapes=list(scratch),
        compiler_params=pltpu.CompilerParams(vmem_limit_bytes=40 * 1024 * 1024),
        cost_estimate=pl.CostEstimate(flops=flops, bytes_accessed=moved, transcendentals=0),
    )(*args)


def ring4(place, shift):
    return lax.bitwise_and(place + shift, 3)


def lanes(start, size):
    return pl.ds(pl.multiple_of(start * size, size), size)


def split3(vals):
    high = vals.astype(bf16)
    rest = vals - high.astype(f32)
    mid = rest.astype(bf16)
    low = (rest - mid.astype(f32)).astype(bf16)
    return high, mid, low


def iota(dims, dim):
    return lax.broadcasted_iota(jnp.int32, dims, dim)


def pack_kernel(place, x, b, c, decay, q, k, v, *outs):
    y = place[2]
    xbc, (q_same, q_other, kv_own, kv_other) = outs[:4], outs[4:]
    lane = iota((LBLK, 128), 1)
    for s in range(4):
        j = ring4(y, s)
        group = lax.shift_right_logical(j, 1)
        xbc[s][:, 0:SLICE] = x[:, lanes(j, SLICE)]
        xbc[s][:, SLICE : SLICE + NSTATE] = b[:, lanes(group, NSTATE)]
        xbc[s][:, SLICE + NSTATE : SLICE + 2 * NSTATE] = c[:, lanes(group, NSTATE)]
        high, mid, low = split3(decay[:, lanes(j, 128)])
        part = jnp.where(lane < 8, high.astype(f32), jnp.where(lane < 16, mid.astype(f32), low.astype(f32)))
        xbc[s][:, SLICE + 2 * NSTATE :] = part.astype(bf16)
    head = lax.bitwise_and(y, 1)
    other = 1 - head
    q_same[...] = q[:, lanes(head, 4 * HDIM)]
    q_other[...] = q[:, lanes(other, 4 * HDIM)]
    kv_own[:, :HDIM] = k[:, lanes(head, HDIM)]
    kv_own[:, HDIM:] = v[:, lanes(head, HDIM)]
    kv_other[:, :HDIM] = k[:, lanes(other, HDIM)]
    kv_other[:, HDIM:] = v[:, lanes(other, HDIM)]


def block_decays(decay_parts):
    tri = (iota((LBLK, LBLK), 0) >= iota((LBLK, LBLK), 1)).astype(f32).astype(bf16)
    cum_parts = jnp.dot(tri, decay_parts, preferred_element_type=f32)
    row = iota((128, SLICE), 0)
    spread = jnp.where(
        (lax.bitwise_and(row, 7) == lax.shift_right_logical(iota((128, SLICE), 1), 6)) & (row < 24), 1.0, 0.0
    )
    return tri, cum_parts, jnp.dot(cum_parts, spread, precision=HIGHEST, preferred_element_type=f32)


def block_sum(block, cum):
    last = cum[LBLK - 1 : LBLK, :]
    decayed = (block[:, 0:SLICE].astype(f32) * jnp.exp(last - cum)).astype(bf16)
    state = lax.dot_general(
        block[:, SLICE : SLICE + NSTATE], decayed, (((0,), (0,)), ((), ())), preferred_element_type=f32
    )
    return state, last


def write_total(out, state, log_total):
    out[0:NSTATE, :] = state.astype(bf16)
    high, mid, low = split3(log_total)
    row = iota((16, log_total.shape[1]), 0)
    out[NSTATE:, :] = jnp.where(
        row == 0,
        high.astype(f32),
        jnp.where(row == 1, mid.astype(f32), jnp.where(row == 2, low.astype(f32), 0.0)),
    ).astype(bf16)


def read_total(vals):
    tail = vals[NSTATE:, :].astype(f32)
    return vals[0:NSTATE, :].astype(f32), tail[0:1] + tail[1:2] + tail[2:3]


def total_kernel(place, r0, r1, r2, r3, t0, t1, t2, t3, ordered, total):
    x, y = place[1], place[2]
    for s, r in enumerate((r0, r1, r2, r3)):
        ordered[ring4(y, -s)] = r[...]
    log_total = jnp.zeros((1, SLICE), f32)
    for block in range(4):
        _, _, cum = block_decays(ordered[block, :, SLICE + 2 * NSTATE :])
        state, last = block_sum(ordered[block], cum)
        log_total = log_total + last
        total[...] = state if block == 0 else jnp.exp(last) * total[...] + state
    logs = jnp.broadcast_to(log_total, (8, SLICE))
    ordered_log = logs
    total_log = ordered_log[0:1]
    for s, t in enumerate((t0, t1, t2, t3)):
        j = ring4(x, s)
        log_part = jnp.where(
            j == 0,
            total_log[:, 0:128],
            jnp.where(j == 1, total_log[:, 128:256], jnp.where(j == 2, total_log[:, 256:384], total_log[:, 384:512])),
        )
        write_total(t, total[:, lanes(j, 128)], log_part)


def plane_kernel(place, r0, r1, r2, r3, out, ordered):
    x = place[1]
    for s, r in enumerate((r0, r1, r2, r3)):
        ordered[ring4(x, -s)] = r[...]
    total, log_total = read_total(ordered[0])
    for block in range(1, 4):
        state, last = read_total(ordered[block])
        total = jnp.exp(last) * total + state
        log_total = log_total + last
    write_total(out, total, log_total)


def entering_kernel(place, r0, r1, r2, r3, up1, up2, up3, g0, g1, g2, g3, ordered, entering):
    x = place[1]
    for s, r in enumerate((r0, r1, r2, r3)):
        ordered[ring4(x, -s)] = r[...]
    current, _ = read_total(up3[...])
    for up in (up2, up1):
        state, last = read_total(up[...])
        current = jnp.exp(last) * current + state
    for block in range(4):
        entering[block] = current.astype(bf16)
        if block < 3:
            state, last = read_total(ordered[block])
            current = jnp.exp(last) * current + state
    for s, g in enumerate((g0, g1, g2, g3)):
        g[...] = entering[ring4(x, s)]


def mixed_kernel(place, r0, r1, r2, r3, g0, g1, g2, g3, skip, m0, m1, m2, m3, ordered, carried, results):
    x, y = place[1], place[2]
    for s, r in enumerate((r0, r1, r2, r3)):
        ordered[ring4(y, -s)] = r[...]
    for s, g in enumerate((g0, g1, g2, g3)):
        carried[:, lanes(ring4(x, -s), 128)] = g[...].astype(f32)
    gain = skip[:, lanes(y, SLICE)]
    causal = iota((LBLK, LBLK), 0) >= iota((LBLK, LBLK), 1)
    low_half = iota((LBLK, 128), 1) < MHDIM
    for block in range(4):
        vals = ordered[block]
        decay_parts = vals[:, SLICE + 2 * NSTATE :]
        tri, cum_parts, cum = block_decays(decay_parts)
        row_parts = lax.dot_general(decay_parts, tri, (((0,), (1,)), ((), ())), preferred_element_type=f32)
        cum_rows = row_parts[0:8] + row_parts[8:16] + row_parts[16:24]
        cum_cols = cum_parts[:, 0:8] + cum_parts[:, 8:16] + cum_parts[:, 16:24]
        write, read = vals[:, SLICE : SLICE + NSTATE], vals[:, SLICE + NSTATE : SLICE + 2 * NSTATE]
        pair_dots = lax.dot_general(read, write, (((1,), (1,)), ((), ())), preferred_element_type=f32)
        held = carried[...]
        held_high = held.astype(bf16)
        held_low = (held - held_high.astype(f32)).astype(bf16)
        inflow = jnp.dot(read, held_high, preferred_element_type=f32) + jnp.dot(
            read, held_low, preferred_element_type=f32
        )
        for pair in range(4):
            part = slice(pair * 128, pair * 128 + 128)
            xs = vals[:, part]
            locals_ = []
            for head in (2 * pair, 2 * pair + 1):
                gap = cum_cols[:, head : head + 1] - cum_rows[head : head + 1, :]
                decays = jnp.exp(jnp.where(causal, gap, neg_large))
                weight = (decays * pair_dots).astype(bf16)
                locals_.append(jnp.dot(weight, xs, preferred_element_type=f32))
            local = jnp.where(low_half, locals_[0], locals_[1])
            mixed = local + jnp.exp(cum[:, part]) * inflow[:, part] + gain[:, part] * xs.astype(f32)
            results[block, :, part] = mixed.astype(bf16)
        if block < 3:
            state, last = block_sum(vals, cum)
            carried[...] = jnp.exp(last) * held + state
    for s, m in enumerate((m0, m1, m2, m3)):
        m[...] = results[ring4(y, s)]


def norm_kernel(place, m0, m1, m2, m3, gate, gain, out):
    y = place[2]
    gated, squares, groups, slots = [], [], [], []
    for s, m in enumerate((m0, m1, m2, m3)):
        j = ring4(y, -s)
        gates = gate[:, lanes(j, SLICE)].astype(f32)
        vals = m[...].astype(f32) * (gates / (1.0 + jnp.exp(-gates)))
        gated.append(vals)
        squares.append(jnp.sum(vals * vals, axis=1, keepdims=True))
        groups.append(lax.shift_right_logical(j, 1))
        slots.append(j)
    for s in range(4):
        total = jnp.zeros((LBLK, 1), f32)
        for other in range(4):
            total = total + jnp.where(groups[other] == groups[s], squares[other], 0.0)
        factor = lax.rsqrt(total * (1.0 / 1024.0) + eps_norm)
        out[:, lanes(slots[s], SLICE)] = (gated[s] * factor * gain[:, lanes(slots[s], SLICE)]).astype(bf16)


def attend(tile, q, keys, values, tops, sums, acc, masks=None):
    rows = pl.ds(pl.multiple_of(tile * TILE, TILE), TILE)
    queries = q[rows, :]
    scores = [
        lax.dot_general(queries, key, (((1,), (1,)), ((), ())), preferred_element_type=f32) for key in keys
    ]
    if masks is not None:
        scores = [jnp.where(mask, score, neg_large) for mask, score in zip(masks, scores)]
    top = functools.reduce(jnp.maximum, scores)
    held_top = tops[rows, 0:1]
    new_top = jnp.maximum(held_top, jnp.max(top, axis=1, keepdims=True))
    expos = [jnp.exp2((score - new_top) * score_scale) for score in scores]
    if masks is not None:
        expos = [jnp.where(mask, expo, 0.0) for mask, expo in zip(masks, expos)]
    factor = jnp.exp2((held_top - new_top) * score_scale)
    total = jnp.sum(functools.reduce(jnp.add, expos), axis=1, keepdims=True)
    summed = functools.reduce(
        jnp.add,
        [jnp.dot(expo.astype(bf16), value, preferred_element_type=f32) for expo, value in zip(expos, values)],
    )
    tops[rows, :] = jnp.broadcast_to(new_top, (TILE, 128))
    sums[rows, :] = jnp.broadcast_to(sums[rows, 0:1] * factor + total, (TILE, 128))
    acc[rows, :] = acc[rows, :] * factor + summed


def own_kernel(place, q0, q1, q2, q3, kv_own, kv_recv, q, tops, sums, acc):
    y = place[2]
    for s, part in enumerate((q0, q1, q2, q3)):
        for head in range(4):
            start = (s * 4 + head) * LBLK
            q[start : start + LBLK, :] = part[:, head * HDIM : (head + 1) * HDIM]
    tops[...] = jnp.full(tops.shape, neg_large, f32)
    sums[...] = jnp.zeros(sums.shape, f32)
    acc[...] = jnp.zeros(acc.shape, f32)
    keys = [kv_own[:, :HDIM], kv_recv[:, :HDIM]]
    values = [kv_own[:, HDIM:], kv_recv[:, HDIM:]]

    def step(tile, _):
        block = ring4(y, -lax.shift_right_logical(tile, 1))
        query_pos = block * LBLK + lax.bitwise_and(iota((TILE, LBLK), 0), LBLK - 1)
        key_pos = iota((TILE, LBLK), 1)
        masks = [key_pos + y * LBLK <= query_pos, key_pos + lax.bitwise_xor(y, 1) * LBLK <= query_pos]
        attend(tile, q, keys, values, tops, sums, acc, masks)
        return 0

    lax.fori_loop(0, q.shape[0] // TILE, step, 0)


def copy_state(old, new):
    for old_ref, new_ref in zip(old, new):
        new_ref[...] = old_ref[...]


def row_kernel(place, q, tops, sums, acc, kv1, kv2, kv3, new_tops, new_sums, new_acc):
    x = place[1]
    copy_state((tops, sums, acc), (new_tops, new_sums, new_acc))
    for s, kv in enumerate((kv1, kv2, kv3)):

        @pl.when(ring4(x, -(s + 1)) < x)
        def _(kv=kv):
            def step(tile, _):
                attend(tile, q, [kv[:, :HDIM]], [kv[:, HDIM:]], new_tops, new_sums, new_acc)
                return 0

            lax.fori_loop(0, q.shape[0] // TILE, step, 0)


def plane_attend(distance, place, q, tops, sums, acc, kv0, kv1, kv2, kv3, new_tops, new_sums, new_acc):
    copy_state((tops, sums, acc), (new_tops, new_sums, new_acc))

    @pl.when(place[0] >= distance)
    def _():
        blocks = (kv0, kv1, kv2, kv3)

        def step(tile, _):
            attend(
                tile,
                q,
                [kv[:, :HDIM] for kv in blocks],
                [kv[:, HDIM:] for kv in blocks],
                new_tops,
                new_sums,
                new_acc,
            )
            return 0

        lax.fori_loop(0, q.shape[0] // TILE, step, 0)


def finish_kernel(place, tops, sums, acc, o0, o1, o2, o3):
    lane = iota((LBLK, 128), 1)
    for s, o in enumerate((o0, o1, o2, o3)):
        stats = jnp.zeros((LBLK, 128), f32)
        for head in range(4):
            start = (s * 4 + head) * LBLK
            rows = slice(start, start + LBLK)
            total = sums[rows, :]
            o[:, head * HDIM : (head + 1) * HDIM] = (acc[rows, :] / jnp.where(total > 0, total, 1.0)).astype(bf16)
            for place_in, part in enumerate(split3(tops[rows, :]) + split3(total)):
                stats = jnp.where(lane == head * 6 + place_in, part.astype(f32), stats)
        o[:, 4 * HDIM :] = stats.astype(bf16)


def merge_kernel(place, o0, o1, o2, o3, out):
    head_group = lax.bitwise_and(place[2], 1)
    for pair, group in (((o0, o2), head_group), ((o1, o3), 1 - head_group)):
        merged = []
        stats = [part[:, 4 * HDIM :].astype(f32) for part in pair]
        for head in range(4):
            tops, sums = [], []
            for stat in stats:
                cols = [stat[:, head * 6 + i : head * 6 + i + 1] for i in range(6)]
                tops.append(cols[0] + cols[1] + cols[2])
                sums.append(cols[3] + cols[4] + cols[5])
            top = jnp.maximum(tops[0], tops[1])
            weights = [total * jnp.exp2((one - top) * score_scale) for one, total in zip(tops, sums)]
            whole = weights[0] + weights[1]
            vals = [part[:, head * HDIM : (head + 1) * HDIM].astype(f32) for part in pair]
            merged.append((vals[0] * (weights[0] / whole) + vals[1] * (weights[1] / whole)).astype(bf16))
        out[:, lanes(group, 4 * HDIM)] = jnp.concatenate(merged, axis=1)


def shift_y(vals, shift):
    return lax.ppermute(vals, "ctx", [(i, (i & ~3) | ((i + shift) & 3)) for i in range(64)])


def shift_x(vals, shift):
    return lax.ppermute(vals, "ctx", [(i, (i & ~12) | ((i + 4 * shift) & 12)) for i in range(64)])


def up_z(vals, shift):
    return lax.ppermute(vals, "ctx", [(i, i + 16 * shift) for i in range(64 - 16 * shift)])


def on_device(
    step_inputs, log_decay, write_vecs, read_vecs, gate_vals, skip_gain, norm_gain, query_rows, key_rows, value_rows
):
    index = lax.axis_index("ctx").astype(jnp.int32)
    place = jnp.stack([index // 16, (index // 4) % 4, index % 4, index])
    decay_copies = jnp.tile(log_decay.reshape(LBLK, 4, 1, 8), (1, 1, 3, 1)).reshape(LBLK, 4, 24)
    decay_grid = jnp.pad(decay_copies, ((0, 0), (0, 0), (0, 104))).reshape(LBLK, 512)
    skip = jnp.repeat(skip_gain, MHDIM).reshape(1, 4 * SLICE)
    gain = norm_gain.reshape(1, 4 * SLICE)

    width = SLICE + 2 * NSTATE + 128
    packed = run(
        pack_kernel,
        [shape((LBLK, width), bf16)] * 4 + [shape((LBLK, 4 * HDIM), bf16)] * 2 + [shape((LBLK, KVW), bf16)] * 2,
        (place, step_inputs, write_vecs, read_vecs, decay_grid, query_rows, key_rows, value_rows),
        moved=3 << 20,
    )
    xbc, (q_same, q_other, kv_own, kv_other) = packed[:4], packed[4:]
    kv_recv = lax.ppermute(kv_other, "ctx", [(i, i ^ 1) for i in range(64)])
    blocks = [xbc[0]] + [shift_y(xbc[s], s) for s in (1, 2, 3)]
    queries = [q_same, shift_y(q_other, 1), shift_y(q_same, 2), shift_y(q_other, 3)]

    kv = jnp.concatenate([kv_own, kv_recv], axis=0)
    planes = [kv] + [up_z(kv, s) for s in (1, 2, 3)]
    columns = [[one] + [shift_x(one, s) for s in (1, 2, 3)] for one in planes]

    totals = run(
        total_kernel,
        [shape((NSTATE + 16, 128), bf16)] * 4,
        (place, *blocks),
        [pltpu.VMEM((4, LBLK, width), bf16), pltpu.VMEM((NSTATE, SLICE), f32)],
        flops=600 << 20,
        moved=2 << 20,
    )
    totals = [totals[0]] + [shift_x(totals[s], s) for s in (1, 2, 3)]
    (plane_total,) = run(
        plane_kernel,
        [shape((NSTATE + 16, 128), bf16)],
        (place, *totals),
        [pltpu.VMEM((4, NSTATE + 16, 128), bf16)],
        moved=1 << 20,
    )
    ups = [up_z(plane_total, s) for s in (1, 2, 3)]
    entering = run(
        entering_kernel,
        [shape((NSTATE, 128), bf16)] * 4,
        (place, *totals, *ups),
        [pltpu.VMEM((4, NSTATE + 16, 128), bf16), pltpu.VMEM((4, NSTATE, 128), bf16)],
        moved=1 << 20,
    )
    entering = [entering[0]] + [shift_x(entering[s], s) for s in (1, 2, 3)]
    mixed = run(
        mixed_kernel,
        [shape((LBLK, SLICE), bf16)] * 4,
        (place, *blocks, *entering, skip),
        [
            pltpu.VMEM((4, LBLK, width), bf16),
            pltpu.VMEM((NSTATE, SLICE), f32),
            pltpu.VMEM((4, LBLK, SLICE), bf16),
        ],
        flops=2 << 30,
        moved=4 << 20,
    )
    mixed = [mixed[0]] + [shift_y(mixed[s], s) for s in (1, 2, 3)]
    (mamba_out,) = run(
        norm_kernel, [shape((LBLK, 4 * SLICE), bf16)], (place, *mixed, gate_vals, gain), moved=4 << 20
    )

    rows = 16 * LBLK
    state_shapes = [shape((rows, 128), f32)] * 3
    unit = 4 * rows * KVW * HDIM
    q, *state = run(
        own_kernel,
        [shape((rows, HDIM), bf16)] + state_shapes,
        (place, *queries, kv_own, kv_recv),
        flops=8 * unit,
        moved=8 << 20,
    )
    state = run(row_kernel, state_shapes, (place, q, *state, *columns[0][1:]), flops=24 * unit, moved=8 << 20)
    for distance in (1, 2, 3):
        state = run(
            functools.partial(plane_attend, distance),
            state_shapes,
            (place, q, *state, *columns[distance]),
            flops=32 * unit,
            moved=8 << 20,
        )
    outs = run(finish_kernel, [shape((LBLK, 4 * HDIM + 128), bf16)] * 4, (place, *state), moved=4 << 20)
    outs = [outs[0]] + [shift_y(outs[s], -s) for s in (1, 2, 3)]
    (attn_out,) = run(merge_kernel, [shape((LBLK, 8 * HDIM), bf16)], (place, *outs), moved=2 << 20)
    return (mamba_out, attn_out)


def solution(mesh):
    in_specs = (
        P("ctx", "tp"),
        P("ctx", "tp"),
        P("ctx", "tp"),
        P("ctx", "tp"),
        P("ctx", "tp"),
        P("tp"),
        P("tp"),
        P("ctx", "tp"),
        P("ctx", "tp"),
        P("ctx", "tp"),
    )
    out_specs = (P("ctx", "tp"), P("ctx", "tp"))
    return jax.shard_map(on_device, mesh=mesh, in_specs=in_specs, out_specs=out_specs, check_vma=False)
```

time: 2200 us -> 127 us (0.06)
  the two profiles are of different devices: /device:TPU:254 before, /device:TPU:104 now
where the time goes in v1:
time: 127 us
  starting transfers between devices  61.4 us (48%)
  Pallas kernels  42.2 us (33%)
  waiting for transfers between devices  18.5 us (15%)
  local copies, waits for them, and re-layouts  3.51 us (3%)
    pallas_call x13, Pallas kernels, run(): pl.pallas_call(kernel, out_shape=outs, in_specs=[smem] + [vmem] * (len(ar...  42.2 us
    ppermute x18, starting transfers between devices, shift_x(): lax.ppermute(vals, 'ctx', [(i, i & ~12 | i + 4 * shift & 12) for i in ran...  34.9 us
    ppermute x12, starting transfers between devices, shift_y(): lax.ppermute(vals, 'ctx', [(i, i & ~3 | i + shift & 3) for i in range(64)])  16.7 us
    ppermute x1, waiting for transfers between devices, on_device(): kv_recv = lax.ppermute(kv_other, 'ctx', [(i, i ^ 1) for i in range(64)])  12.4 us
    ppermute x6, starting transfers between devices, up_z(): lax.ppermute(vals, 'ctx', [(i, i + 16 * shift) for i in range(64 - 16 * s...  7.72 us
    unnamed x21, local copies, waits for them, and re-layouts  3.2 us
    ppermute x12, waiting for transfers between devices, shift_y(): lax.ppermute(vals, 'ctx', [(i, i & ~3 | i + shift & 3) for i in range(64)])  2.93 us
  transfers between devices with their start and end apart: 37, of which 5 were waited for; matrix products, arithmetic and copies ran while one was open for 0% of the time, Pallas kernels for 31%

profile of v1, /device:TPU:104, one launch (start us, length us, event | category | flops | bytes accessed | tf_op | source)
XLA Modules:
  0.0 126.6 jit_solution(3721721978945355432)
XLA Ops:
  2.4 0.9 copy-done.5
  3.3 0.8 copy-done.7
  4.2 0.7 shard_map.113
  4.8 1.7 %collective-permute-start = (bf16[128,1152]{1,0:T(8,128)(2,1)S(1)}, bf16[128,1152]{1,0:T(8,128)(2,1)S(1)}, u32[]{:S(2)}, u32[]{:S(2)}) collective-permute-start(bf16[128,1152]{1,0:T(8,128)(2,1)S(1)} %get-tuple-element.43), channel_id=1, source_target_pairs={{0,4},{4,8},{8,12},{12,0},{16,20},{20,24},{24,28},{28,16},{32,36},... | collective-permute-start | bytes 884744 | tf_op jit(solution)/shard_map/ppermute | solution.py:360
  6.5 0.9 collective-permute-start.1
  7.5 2.4 %collective-permute-start.2 = (bf16[128,1152]{1,0:T(8,128)(2,1)S(1)}, bf16[128,1152]{1,0:T(8,128)(2,1)S(1)}, u32[]{:S(2)}, u32[]{:S(2)}) collective-permute-start(bf16[128,1152]{1,0:T(8,128)(2,1)S(1)} %get-tuple-element.45), channel_id=1, source_target_pairs={{0,12},{4,0},{8,4},{12,8},{16,28},{20,16},{24,20},{28,24},{32,44},... | collective-permute-start | bytes 884744 | tf_op jit(solution)/shard_map/ppermute | solution.py:360
  9.9 2.0 %collective-permute-start.18 = (bf16[128,256]{1,0:T(8,128)(2,1)S(1)}, bf16[128,256]{1,0:T(8,128)(2,1)S(1)}, u32[]{:S(2)}, u32[]{:S(2)}) collective-permute-start(bf16[128,256]{1,0:T(8,128)(2,1)S(1)} %get-tuple-element.61), channel_id=1, source_target_pairs={{0,4},{4,0},{8,12},{12,8},{16,20},{20,16},{24,28},{28,24},{32,36},... | collective-permute-start | bytes 196616 | tf_op jit(solution)/shard_map/ppermute | solution.py:389
  11.9 12.4 %collective-permute-done.18.kv_recv = bf16[128,256]{1,0:T(8,128)(2,1)S(1)} collective-permute-done((bf16[128,256]{1,0:T(8,128)(2,1)S(1)}, bf16[128,256]{1,0:T(8,128)(2,1)S(1)}, u32[]{:S(2)}, u32[]{:S(2)}) %collective-permute-start.18) | collective-permute-done | bytes 65568 | tf_op jit(solution)/shard_map/ppermute | solution.py:389
  24.3 2.5 %collective-permute-start.16 = (bf16[128,512]{1,0:T(8,128)(2,1)S(1)}, bf16[128,512]{1,0:T(8,128)(2,1)S(1)}, u32[]{:S(2)}, u32[]{:S(2)}) collective-permute-start(bf16[128,512]{1,0:T(8,128)(2,1)S(1)} %get-tuple-element.58.q0), channel_id=1, source_target_pairs={{0,8},{4,12},{8,0},{12,4},{16,24},{20,28},{24,16},{28,20},{32,40},... | collective-permute-start | bytes 393224 | tf_op jit(solution)/shard_map/ppermute | solution.py:360
  27.0 1.5 %collective-permute-start.19 = (bf16[256,256]{1,0:T(8,128)(2,1)S(1)}, bf16[256,256]{1,0:T(8,128)(2,1)S(1)}, u32[]{:S(2)}, u32[]{:S(2)}) collective-permute-start(bf16[256,256]{1,0:T(8,128)(2,1)S(1)} %constant_dynamic-update-slice_fusion), channel_id=1, source_target_pairs={{0,16},{4,20},{8,24},{12,28},{16,32},{20,36},{24,40},{28,44},{32,4... | collective-permute-start | bytes 393224 | tf_op jit(solution)/shard_map/ppermute | solution.py:364
  28.5 2.7 %collective-permute-start.20 = (bf16[256,256]{1,0:T(8,128)(2,1)S(1)}, bf16[256,256]{1,0:T(8,128)(2,1)S(1)}, u32[]{:S(2)}, u32[]{:S(2)}) collective-permute-start(bf16[256,256]{1,0:T(8,128)(2,1)S(1)} %constant_dynamic-update-slice_fusion), channel_id=1, source_target_pairs={{0,32},{4,36},{8,40},{12,44},{16,48},{20,52},{24,56},{28,60},{32,0... | collective-permute-start | bytes 393224 | tf_op jit(solution)/shard_map/ppermute | solution.py:364
  31.4 3.1 %shard_map.114 = (bf16[272,128]{1,0:T(8,128)(2,1)S(1)}, bf16[272,128]{1,0:T(8,128)(2,1)S(1)}, bf16[272,128]{1,0:T(8,128)(2,1)S(1)}, bf16[272,128]{1,0:T(8,128)(2,1)S(1)}) custom-call(s32[4]{0:T(128)S(1)} %pad_add_fusion.place, bf16[128,1152]{1,0:T(8,128)(2,1)S(1)} %get-tuple-element.42.r0, bf16[128,1152]{1,0:T(8,128)(2,1)S(1)} %collective-permute-done.r1, ...), custom_call_target="tpu_custom_call" | custom-call | flops 629145600 | bytes 2097152 | tf_op jit(solution)/shard_map/pallas_call | solution.py:34
  34.6 1.5 %collective-permute-start.21 = (bf16[256,256]{1,0:T(8,128)(2,1)S(1)}, bf16[256,256]{1,0:T(8,128)(2,1)S(1)}, u32[]{:S(2)}, u32[]{:S(2)}) collective-permute-start(bf16[256,256]{1,0:T(8,128)(2,1)S(1)} %constant_dynamic-update-slice_fusion), channel_id=1, source_target_pairs={{0,48},{4,52},{8,56},{12,60},{16,0},{20,4},{24,8},{28,12},{32,16},... | collective-permute-start | bytes 393224 | tf_op jit(solution)/shard_map/ppermute | solution.py:364
  36.1 1.3 %collective-permute-start.22 = (bf16[256,256]{1,0:T(8,128)(2,1)S(1)}, bf16[256,256]{1,0:T(8,128)(2,1)S(1)}, u32[]{:S(2)}, u32[]{:S(2)}) collective-permute-start(bf16[256,256]{1,0:T(8,128)(2,1)S(1)} %constant_dynamic-update-slice_fusion), channel_id=1, source_target_pairs={{0,64},{4,68},{8,72},{12,76},{16,80},{20,84},{24,88},{28,92},{32,9... | collective-permute-start | bytes 393224 | tf_op jit(solution)/shard_map/ppermute | solution.py:368
  37.4 1.3 %collective-permute-start.26 = (bf16[256,256]{1,0:T(8,128)(2,1)S(1)}, bf16[256,256]{1,0:T(8,128)(2,1)S(1)}, u32[]{:S(2)}, u32[]{:S(2)}) collective-permute-start(bf16[256,256]{1,0:T(8,128)(2,1)S(1)} %constant_dynamic-update-slice_fusion), channel_id=1, source_target_pairs={{0,128},{4,132},{8,136},{12,140},{16,144},{20,148},{24,152},{28,15... | collective-permute-start | bytes 393224 | tf_op jit(solution)/shard_map/ppermute | solution.py:368
  39.4 0.9 collective-permute-start.4
  40.3 5.4 %shard_map.119 = (bf16[2048,128]{1,0:T(8,128)(2,1)S(1)}, f32[2048,128]{1,0:T(8,128)S(1)}, f32[2048,128]{1,0:T(8,128)S(1)}, f32[2048,128]{1,0:T(8,128)S(1)}) custom-call(s32[4]{0:T(128)S(1)} %pad_add_fusion.place, bf16[128,512]{1,0:T(8,128)(2,1)S(1)} %get-tuple-element.58.q0, bf16[128,512]{1,0:T(8,128)(2,1)S(1)} %collective-permute-done.15.q1, ...), custom_call_target="tpu_custom_call" | custom-call | flops 2147483648 | bytes 8388608 | tf_op jit(solution)/shard_map/pallas_call | solution.py:34
  45.7 1.3 %collective-permute-start.30 = (bf16[256,256]{1,0:T(8,128)(2,1)S(1)}, bf16[256,256]{1,0:T(8,128)(2,1)S(1)}, u32[]{:S(2)}, u32[]{:S(2)}) collective-permute-start(bf16[256,256]{1,0:T(8,128)(2,1)S(1)} %constant_dynamic-update-slice_fusion), channel_id=1, source_target_pairs={{0,192},{4,196},{8,200},{12,204},{16,208},{20,212},{24,216},{28,22... | collective-permute-start | bytes 393224 | tf_op jit(solution)/shard_map/ppermute | solution.py:368
  47.0 2.7 %collective-permute-start.23 = (bf16[256,256]{1,0:T(8,128)(2,1)S(1)}, bf16[256,256]{1,0:T(8,128)(2,1)S(1)}, u32[]{:S(2)}, u32[]{:S(2)}) collective-permute-start(bf16[256,256]{1,0:T(8,128)(2,1)S(1)} %collective-permute-done.22.kv0), channel_id=1, source_target_pairs={{0,16},{4,20},{8,24},{12,28},{16,32},{20,36},{24,40},{28,44},{32,4... | collective-permute-start | bytes 393224 | tf_op jit(solution)/shard_map/ppermute | solution.py:364
  49.7 0.7 collective-permute-start.24
  50.4 2.2 %collective-permute-start.25 = (bf16[256,256]{1,0:T(8,128)(2,1)S(1)}, bf16[256,256]{1,0:T(8,128)(2,1)S(1)}, u32[]{:S(2)}, u32[]{:S(2)}) collective-permute-start(bf16[256,256]{1,0:T(8,128)(2,1)S(1)} %collective-permute-done.22.kv0), channel_id=1, source_target_pairs={{0,48},{4,52},{8,56},{12,60},{16,0},{20,4},{24,8},{28,12},{32,16},... | collective-permute-start | bytes 393224 | tf_op jit(solution)/shard_map/ppermute | solution.py:364
  52.7 1.1 collective-permute-start.5
  53.8 0.8 shard_map.120
  54.6 2.4 %collective-permute-done.5.r3 = bf16[272,128]{1,0:T(8,128)(2,1)S(1)} collective-permute-done((bf16[272,128]{1,0:T(8,128)(2,1)S(1)}, bf16[272,128]{1,0:T(8,128)(2,1)S(1)}, u32[]{:S(2)}, u32[]{:S(2)}) %collective-permute-start.5) | collective-permute-done | bytes 69664 | tf_op jit(solution)/shard_map/ppermute | solution.py:364
  57.0 2.7 %collective-permute-start.27 = (bf16[256,256]{1,0:T(8,128)(2,1)S(1)}, bf16[256,256]{1,0:T(8,128)(2,1)S(1)}, u32[]{:S(2)}, u32[]{:S(2)}) collective-permute-start(bf16[256,256]{1,0:T(8,128)(2,1)S(1)} %collective-permute-done.26.kv0), channel_id=1, source_target_pairs={{0,16},{4,20},{8,24},{12,28},{16,32},{20,36},{24,40},{28,44},{32,4... | collective-permute-start | bytes 393224 | tf_op jit(solution)/shard_map/ppermute | solution.py:364
  60.4 9.1 %collective-permute-start.28 = (bf16[256,256]{1,0:T(8,128)(2,1)S(1)}, bf16[256,256]{1,0:T(8,128)(2,1)S(1)}, u32[]{:S(2)}, u32[]{:S(2)}) collective-permute-start(bf16[256,256]{1,0:T(8,128)(2,1)S(1)} %collective-permute-done.26.kv0), channel_id=1, source_target_pairs={{0,32},{4,36},{8,40},{12,44},{16,48},{20,52},{24,56},{28,60},{32,0... | collective-permute-start | bytes 393224 | tf_op jit(solution)/shard_map/ppermute | solution.py:364
  69.4 2.0 %collective-permute-start.31 = (bf16[256,256]{1,0:T(8,128)(2,1)S(1)}, bf16[256,256]{1,0:T(8,128)(2,1)S(1)}, u32[]{:S(2)}, u32[]{:S(2)}) collective-permute-start(bf16[256,256]{1,0:T(8,128)(2,1)S(1)} %collective-permute-done.30.kv0), channel_id=1, source_target_pairs={{0,16},{4,20},{8,24},{12,28},{16,32},{20,36},{24,40},{28,44},{32,4... | collective-permute-start | bytes 393224 | tf_op jit(solution)/shard_map/ppermute | solution.py:364
  71.5 1.3 %collective-permute-start.6 = (bf16[272,128]{1,0:T(8,128)(2,1)S(1)}, bf16[272,128]{1,0:T(8,128)(2,1)S(1)}, u32[]{:S(2)}, u32[]{:S(2)}) collective-permute-start(bf16[272,128]{1,0:T(8,128)(2,1)S(1)} %shard_map.115), channel_id=1, source_target_pairs={{0,64},{4,68},{8,72},{12,76},{16,80},{20,84},{24,88},{28,92},{32,9... | collective-permute-start | bytes 208904 | tf_op jit(solution)/shard_map/ppermute | solution.py:368
  72.8 7.1 %shard_map.121 = (f32[2048,128]{1,0:T(8,128)S(1)}, f32[2048,128]{1,0:T(8,128)S(1)}, f32[2048,128]{1,0:T(8,128)S(1)}) custom-call(s32[4]{0:T(128)S(1)} %pad_add_fusion.place, bf16[2048,128]{1,0:T(8,128)(2,1)S(1)} %get-tuple-element.62.q, f32[2048,128]{1,0:T(8,128)S(1)} %get-tuple-element.66.tops, f32[2048,128]{1,0:T(8,128)S(1)} %get-tuple-element.67.sums, ...), custom_call_target="tpu_custom_call" | custom-call | flops 8589934592 | bytes 8388608 | tf_op jit(solution)/shard_map/pallas_call | solution.py:34
  80.1 2.6 %collective-permute-start.33 = (bf16[256,256]{1,0:T(8,128)(2,1)S(1)}, bf16[256,256]{1,0:T(8,128)(2,1)S(1)}, u32[]{:S(2)}, u32[]{:S(2)}) collective-permute-start(bf16[256,256]{1,0:T(8,128)(2,1)S(1)} %collective-permute-done.30.kv0), channel_id=1, source_target_pairs={{0,48},{4,52},{8,56},{12,60},{16,0},{20,4},{24,8},{28,12},{32,16},... | collective-permute-start | bytes 393224 | tf_op jit(solution)/shard_map/ppermute | solution.py:364
  82.7 1.3 %collective-permute-start.7 = (bf16[272,128]{1,0:T(8,128)(2,1)S(1)}, bf16[272,128]{1,0:T(8,128)(2,1)S(1)}, u32[]{:S(2)}, u32[]{:S(2)}) collective-permute-start(bf16[272,128]{1,0:T(8,128)(2,1)S(1)} %shard_map.115), channel_id=1, source_target_pairs={{0,128},{4,132},{8,136},{12,140},{16,144},{20,148},{24,152},{28,15... | collective-permute-start | bytes 208904 | tf_op jit(solution)/shard_map/ppermute | solution.py:368
  84.0 1.3 %collective-permute-start.8 = (bf16[272,128]{1,0:T(8,128)(2,1)S(1)}, bf16[272,128]{1,0:T(8,128)(2,1)S(1)}, u32[]{:S(2)}, u32[]{:S(2)}) collective-permute-start(bf16[272,128]{1,0:T(8,128)(2,1)S(1)} %shard_map.115), channel_id=1, source_target_pairs={{0,192},{4,196},{8,200},{12,204},{16,208},{20,212},{24,216},{28,22... | collective-permute-start | bytes 208904 | tf_op jit(solution)/shard_map/ppermute | solution.py:368
  85.3 7.1 %shard_map.122 = (f32[2048,128]{1,0:T(8,128)S(1)}, f32[2048,128]{1,0:T(8,128)S(1)}, f32[2048,128]{1,0:T(8,128)S(1)}) custom-call(s32[4]{0:T(128)S(1)} %pad_add_fusion.place, bf16[2048,128]{1,0:T(8,128)(2,1)S(1)} %get-tuple-element.62.q, f32[2048,128]{1,0:T(8,128)S(1)} %get-tuple-element.69.tops, f32[2048,128]{1,0:T(8,128)S(1)} %get-tuple-element.70.sums, ...), custom_call_target="tpu_custom_call" | custom-call | flops 8589934592 | bytes 8388608 | tf_op jit(solution)/shard_map/pallas_call | solution.py:34
  92.5 0.7 collective-permute-done.8.up3
  94.0 2.9 %collective-permute-start.10 = (bf16[256,128]{1,0:T(8,128)(2,1)S(1)}, bf16[256,128]{1,0:T(8,128)(2,1)S(1)}, u32[]{:S(2)}, u32[]{:S(2)}) collective-permute-start(bf16[256,128]{1,0:T(8,128)(2,1)S(1)} %get-tuple-element.52), channel_id=1, source_target_pairs={{0,32},{4,36},{8,40},{12,44},{16,48},{20,52},{24,56},{28,60},{32,0... | collective-permute-start | bytes 196616 | tf_op jit(solution)/shard_map/ppermute | solution.py:364
  96.8 1.3 %collective-permute-start.11 = (bf16[256,128]{1,0:T(8,128)(2,1)S(1)}, bf16[256,128]{1,0:T(8,128)(2,1)S(1)}, u32[]{:S(2)}, u32[]{:S(2)}) collective-permute-start(bf16[256,128]{1,0:T(8,128)(2,1)S(1)} %get-tuple-element.53), channel_id=1, source_target_pairs={{0,48},{4,52},{8,56},{12,60},{16,0},{20,4},{24,8},{28,12},{32,16},... | collective-permute-start | bytes 196616 | tf_op jit(solution)/shard_map/ppermute | solution.py:364
  98.1 7.4 %shard_map.123 = (f32[2048,128]{1,0:T(8,128)S(1)}, f32[2048,128]{1,0:T(8,128)S(1)}, f32[2048,128]{1,0:T(8,128)S(1)}) custom-call(s32[4]{0:T(128)S(1)} %pad_add_fusion.place, bf16[2048,128]{1,0:T(8,128)(2,1)S(1)} %get-tuple-element.62.q, f32[2048,128]{1,0:T(8,128)S(1)} %get-tuple-element.72.tops, f32[2048,128]{1,0:T(8,128)S(1)} %get-tuple-element.73.sums, ...), custom_call_target="tpu_custom_call" | custom-call | flops 8589934592 | bytes 8388608 | tf_op jit(solution)/shard_map/pallas_call | solution.py:34
  105.6 1.4 %shard_map.124 = (bf16[128,640]{1,0:T(8,128)(2,1)S(1)}, bf16[128,640]{1,0:T(8,128)(2,1)S(1)}, bf16[128,640]{1,0:T(8,128)(2,1)S(1)}, bf16[128,640]{1,0:T(8,128)(2,1)S(1)}) custom-call(s32[4]{0:T(128)S(1)} %pad_add_fusion.place, f32[2048,128]{1,0:T(8,128)S(1)} %get-tuple-element.75.tops, f32[2048,128]{1,0:T(8,128)S(1)} %get-tuple-element.76.sums, ...), custom_call_target="tpu_custom_call" | custom-call | flops 1000000 | bytes 4194304 | tf_op jit(solution)/shard_map/pallas_call | solution.py:34
  107.0 2.1 %collective-permute-start.34 = (bf16[128,640]{1,0:T(8,128)(2,1)S(1)}, bf16[128,640]{1,0:T(8,128)(2,1)S(1)}, u32[]{:S(2)}, u32[]{:S(2)}) collective-permute-start(bf16[128,640]{1,0:T(8,128)(2,1)S(1)} %get-tuple-element.79), channel_id=1, source_target_pairs={{0,12},{4,0},{8,4},{12,8},{16,28},{20,16},{24,20},{28,24},{32,44},... | collective-permute-start | bytes 491528 | tf_op jit(solution)/shard_map/ppermute | solution.py:360
  109.1 1.3 %collective-permute-start.35 = (bf16[128,640]{1,0:T(8,128)(2,1)S(1)}, bf16[128,640]{1,0:T(8,128)(2,1)S(1)}, u32[]{:S(2)}, u32[]{:S(2)}) collective-permute-start(bf16[128,640]{1,0:T(8,128)(2,1)S(1)} %get-tuple-element.80), channel_id=1, source_target_pairs={{0,8},{4,12},{8,0},{12,4},{16,24},{20,28},{24,16},{28,20},{32,40},... | collective-permute-start | bytes 491528 | tf_op jit(solution)/shard_map/ppermute | solution.py:360
  110.6 3.7 %shard_map.117 = (bf16[128,512]{1,0:T(8,128)(2,1)S(1)}, bf16[128,512]{1,0:T(8,128)(2,1)S(1)}, bf16[128,512]{1,0:T(8,128)(2,1)S(1)}, bf16[128,512]{1,0:T(8,128)(2,1)S(1)}) custom-call(s32[4]{0:T(128)S(1)} %pad_add_fusion.place, bf16[128,1152]{1,0:T(8,128)(2,1)S(1)} %get-tuple-element.42.r0, bf16[128,1152]{1,0:T(8,128)(2,1)S(1)} %collective-permute-done.r1, ...), custom_call_target="tpu_custom_call" | custom-call | flops 2147483648 | bytes 4194304 | tf_op jit(solution)/shard_map/pallas_call | solution.py:34
  114.4 2.6 %collective-permute-start.12 = (bf16[128,512]{1,0:T(8,128)(2,1)S(1)}, bf16[128,512]{1,0:T(8,128)(2,1)S(1)}, u32[]{:S(2)}, u32[]{:S(2)}) collective-permute-start(bf16[128,512]{1,0:T(8,128)(2,1)S(1)} %get-tuple-element.55), channel_id=1, source_target_pairs={{0,4},{4,8},{8,12},{12,0},{16,20},{20,24},{24,28},{28,16},{32,36},... | collective-permute-start | bytes 393224 | tf_op jit(solution)/shard_map/ppermute | solution.py:360
  117.0 1.3 %collective-permute-start.13 = (bf16[128,512]{1,0:T(8,128)(2,1)S(1)}, bf16[128,512]{1,0:T(8,128)(2,1)S(1)}, u32[]{:S(2)}, u32[]{:S(2)}) collective-permute-start(bf16[128,512]{1,0:T(8,128)(2,1)S(1)} %get-tuple-element.56), channel_id=1, source_target_pairs={{0,8},{4,12},{8,0},{12,4},{16,24},{20,28},{24,16},{28,20},{32,40},... | collective-permute-start | bytes 393224 | tf_op jit(solution)/shard_map/ppermute | solution.py:360
  118.3 1.4 %collective-permute-start.14 = (bf16[128,512]{1,0:T(8,128)(2,1)S(1)}, bf16[128,512]{1,0:T(8,128)(2,1)S(1)}, u32[]{:S(2)}, u32[]{:S(2)}) collective-permute-start(bf16[128,512]{1,0:T(8,128)(2,1)S(1)} %get-tuple-element.57), channel_id=1, source_target_pairs={{0,12},{4,0},{8,4},{12,8},{16,28},{20,16},{24,20},{28,24},{32,44},... | collective-permute-start | bytes 393224 | tf_op jit(solution)/shard_map/ppermute | solution.py:360
  119.7 2.1 %shard_map.125 = bf16[128,1024]{1,0:T(8,128)(2,1)} custom-call(s32[4]{0:T(128)S(1)} %pad_add_fusion.place, bf16[128,640]{1,0:T(8,128)(2,1)S(1)} %get-tuple-element.78.o0, bf16[128,640]{1,0:T(8,128)(2,1)S(1)} %collective-permute-done.34.o1, bf16[128,640]{1,0:T(8,128)(2,1)S(1)} %collective-permute-done.35.o2, bf16[128,640]{1,0:T(8,128)(2,1)S(1)} %collective-permute-done.36.o3), custom_call_target="tpu_custom_call" | custom-call | flops 1000000 | bytes 2097152 | tf_op jit(solution)/shard_map/pallas_call | solution.py:34
  121.8 1.8 %collective-permute-done.13.m2 = bf16[128,512]{1,0:T(8,128)(2,1)S(1)} collective-permute-done((bf16[128,512]{1,0:T(8,128)(2,1)S(1)}, bf16[128,512]{1,0:T(8,128)(2,1)S(1)}, u32[]{:S(2)}, u32[]{:S(2)}) %collective-permute-start.13) | collective-permute-done | bytes 131104 | tf_op jit(solution)/shard_map/ppermute | solution.py:360
  123.6 1.1 collective-permute-done.14.m3
  124.7 1.9 %shard_map.118 = bf16[128,2048]{1,0:T(8,128)(2,1)} custom-call(s32[4]{0:T(128)S(1)} %pad_add_fusion.place, bf16[128,512]{1,0:T(8,128)(2,1)S(1)} %get-tuple-element.54.m0, bf16[128,512]{1,0:T(8,128)(2,1)S(1)} %collective-permute-done.12.m1, bf16[128,512]{1,0:T(8,128)(2,1)S(1)} %collective-permute-done.13.m2, bf16[128,512]{1,0:T(8,128)(2,1)S(1)} %collective-permute-done.14.m3, ...), custom_call_target="tpu_custom_call" | custom-call | flops 1000000 | bytes 4194304 | tf_op jit(solution)/shard_map/pallas_call | solution.py:34
  (67 shorter events, 4.6 us)
Async XLA Ops:
  0.6 0.7 copy-start
  0.6 1.0 copy-start.1
  1.4 1.0 copy-start.3
  1.4 1.0 copy-start.4
  1.4 1.0 copy-start.6
  2.4 0.9 copy-start.5
  3.3 0.8 copy-start.7
  4.8 21.9 %collective-permute-start = (bf16[128,1152]{1,0:T(8,128)(2,1)S(1)}, bf16[128,1152]{1,0:T(8,128)(2,1)S(1)}, u32[]{:S(2)}, u32[]{:S(2)}) collective-permute-start(bf16[128,1152]{1,0:T(8,128)(2,1)S(1)} %get-tuple-element.43), channel_id=1, source_target_pairs={{0,4},{4,8},{8,12},{12,0},{16,20},{20,24},{24,28},{28,16},{32,36},... | collective-permute-start | bytes 884744 | tf_op jit(solution)/shard_map/ppermute | solution.py:360
  6.5 20.5 %collective-permute-start.1 = (bf16[128,1152]{1,0:T(8,128)(2,1)S(1)}, bf16[128,1152]{1,0:T(8,128)(2,1)S(1)}, u32[]{:S(2)}, u32[]{:S(2)}) collective-permute-start(bf16[128,1152]{1,0:T(8,128)(2,1)S(1)} %get-tuple-element.44), channel_id=1, source_target_pairs={{0,8},{4,12},{8,0},{12,4},{16,24},{20,28},{24,16},{28,20},{32,40},... | collective-permute-start | bytes 884744 | tf_op jit(solution)/shard_map/ppermute | solution.py:360
  7.5 21.1 %collective-permute-start.2 = (bf16[128,1152]{1,0:T(8,128)(2,1)S(1)}, bf16[128,1152]{1,0:T(8,128)(2,1)S(1)}, u32[]{:S(2)}, u32[]{:S(2)}) collective-permute-start(bf16[128,1152]{1,0:T(8,128)(2,1)S(1)} %get-tuple-element.45), channel_id=1, source_target_pairs={{0,12},{4,0},{8,4},{12,8},{16,28},{20,16},{24,20},{28,24},{32,44},... | collective-permute-start | bytes 884744 | tf_op jit(solution)/shard_map/ppermute | solution.py:360
  9.9 24.7 %collective-permute-start.15 = (bf16[128,512]{1,0:T(8,128)(2,1)S(1)}, bf16[128,512]{1,0:T(8,128)(2,1)S(1)}, u32[]{:S(2)}, u32[]{:S(2)}) collective-permute-start(bf16[128,512]{1,0:T(8,128)(2,1)S(1)} %get-tuple-element.59), channel_id=1, source_target_pairs={{0,4},{4,8},{8,12},{12,0},{16,20},{20,24},{24,28},{28,16},{32,36},... | collective-permute-start | bytes 393224 | tf_op jit(solution)/shard_map/ppermute | solution.py:360
  9.9 14.4 %collective-permute-start.18 = (bf16[128,256]{1,0:T(8,128)(2,1)S(1)}, bf16[128,256]{1,0:T(8,128)(2,1)S(1)}, u32[]{:S(2)}, u32[]{:S(2)}) collective-permute-start(bf16[128,256]{1,0:T(8,128)(2,1)S(1)} %get-tuple-element.61), channel_id=1, source_target_pairs={{0,4},{4,0},{8,12},{12,8},{16,20},{20,16},{24,28},{28,24},{32,36},... | collective-permute-start | bytes 196616 | tf_op jit(solution)/shard_map/ppermute | solution.py:389
  24.3 7.0 %copy-start.9 = (f32[32]{0:T(128)S(1)}, f32[32]{0:T(128)}, u32[]{:S(2)}) copy-start(f32[32]{0:T(128)} %param.15) | copy-start | bytes 388
  24.3 11.8 %collective-permute-start.16 = (bf16[128,512]{1,0:T(8,128)(2,1)S(1)}, bf16[128,512]{1,0:T(8,128)(2,1)S(1)}, u32[]{:S(2)}, u32[]{:S(2)}) collective-permute-start(bf16[128,512]{1,0:T(8,128)(2,1)S(1)} %get-tuple-element.58.q0), channel_id=1, source_target_pairs={{0,8},{4,12},{8,0},{12,4},{16,24},{20,28},{24,16},{28,20},{32,40},... | collective-permute-start | bytes 393224 | tf_op jit(solution)/shard_map/ppermute | solution.py:360
  26.8 10.6 %collective-permute-start.17 = (bf16[128,512]{1,0:T(8,128)(2,1)S(1)}, bf16[128,512]{1,0:T(8,128)(2,1)S(1)}, u32[]{:S(2)}, u32[]{:S(2)}) collective-permute-start(bf16[128,512]{1,0:T(8,128)(2,1)S(1)} %get-tuple-element.59), channel_id=1, source_target_pairs={{0,12},{4,0},{8,4},{12,8},{16,28},{20,16},{24,20},{28,24},{32,44},... | collective-permute-start | bytes 393224 | tf_op jit(solution)/shard_map/ppermute | solution.py:360
  27.0 11.7 %collective-permute-start.19 = (bf16[256,256]{1,0:T(8,128)(2,1)S(1)}, bf16[256,256]{1,0:T(8,128)(2,1)S(1)}, u32[]{:S(2)}, u32[]{:S(2)}) collective-permute-start(bf16[256,256]{1,0:T(8,128)(2,1)S(1)} %constant_dynamic-update-slice_fusion), channel_id=1, source_target_pairs={{0,16},{4,20},{8,24},{12,28},{16,32},{20,36},{24,40},{28,44},{32,4... | collective-permute-start | bytes 393224 | tf_op jit(solution)/shard_map/ppermute | solution.py:364
  28.5 10.8 %collective-permute-start.20 = (bf16[256,256]{1,0:T(8,128)(2,1)S(1)}, bf16[256,256]{1,0:T(8,128)(2,1)S(1)}, u32[]{:S(2)}, u32[]{:S(2)}) collective-permute-start(bf16[256,256]{1,0:T(8,128)(2,1)S(1)} %constant_dynamic-update-slice_fusion), channel_id=1, source_target_pairs={{0,32},{4,36},{8,40},{12,44},{16,48},{20,52},{24,56},{28,60},{32,0... | collective-permute-start | bytes 393224 | tf_op jit(solution)/shard_map/ppermute | solution.py:364
  34.6 11.1 %collective-permute-start.21 = (bf16[256,256]{1,0:T(8,128)(2,1)S(1)}, bf16[256,256]{1,0:T(8,128)(2,1)S(1)}, u32[]{:S(2)}, u32[]{:S(2)}) collective-permute-start(bf16[256,256]{1,0:T(8,128)(2,1)S(1)} %constant_dynamic-update-slice_fusion), channel_id=1, source_target_pairs={{0,48},{4,52},{8,56},{12,60},{16,0},{20,4},{24,8},{28,12},{32,16},... | collective-permute-start | bytes 393224 | tf_op jit(solution)/shard_map/ppermute | solution.py:364
  36.1 10.9 %collective-permute-start.22 = (bf16[256,256]{1,0:T(8,128)(2,1)S(1)}, bf16[256,256]{1,0:T(8,128)(2,1)S(1)}, u32[]{:S(2)}, u32[]{:S(2)}) collective-permute-start(bf16[256,256]{1,0:T(8,128)(2,1)S(1)} %constant_dynamic-update-slice_fusion), channel_id=1, source_target_pairs={{0,64},{4,68},{8,72},{12,76},{16,80},{20,84},{24,88},{28,92},{32,9... | collective-permute-start | bytes 393224 | tf_op jit(solution)/shard_map/ppermute | solution.py:368
  37.4 12.3 %collective-permute-start.26 = (bf16[256,256]{1,0:T(8,128)(2,1)S(1)}, bf16[256,256]{1,0:T(8,128)(2,1)S(1)}, u32[]{:S(2)}, u32[]{:S(2)}) collective-permute-start(bf16[256,256]{1,0:T(8,128)(2,1)S(1)} %constant_dynamic-update-slice_fusion), channel_id=1, source_target_pairs={{0,128},{4,132},{8,136},{12,140},{16,144},{20,148},{24,152},{28,15... | collective-permute-start | bytes 393224 | tf_op jit(solution)/shard_map/ppermute | solution.py:368
  38.7 11.7 %collective-permute-start.3 = (bf16[272,128]{1,0:T(8,128)(2,1)S(1)}, bf16[272,128]{1,0:T(8,128)(2,1)S(1)}, u32[]{:S(2)}, u32[]{:S(2)}) collective-permute-start(bf16[272,128]{1,0:T(8,128)(2,1)S(1)} %get-tuple-element.47), channel_id=1, source_target_pairs={{0,16},{4,20},{8,24},{12,28},{16,32},{20,36},{24,40},{28,44},{32,4... | collective-permute-start | bytes 208904 | tf_op jit(solution)/shard_map/ppermute | solution.py:364
  39.4 13.3 %collective-permute-start.4 = (bf16[272,128]{1,0:T(8,128)(2,1)S(1)}, bf16[272,128]{1,0:T(8,128)(2,1)S(1)}, u32[]{:S(2)}, u32[]{:S(2)}) collective-permute-start(bf16[272,128]{1,0:T(8,128)(2,1)S(1)} %get-tuple-element.48), channel_id=1, source_target_pairs={{0,32},{4,36},{8,40},{12,44},{16,48},{20,52},{24,56},{28,60},{32,0... | collective-permute-start | bytes 208904 | tf_op jit(solution)/shard_map/ppermute | solution.py:364
  45.7 14.6 %collective-permute-start.30 = (bf16[256,256]{1,0:T(8,128)(2,1)S(1)}, bf16[256,256]{1,0:T(8,128)(2,1)S(1)}, u32[]{:S(2)}, u32[]{:S(2)}) collective-permute-start(bf16[256,256]{1,0:T(8,128)(2,1)S(1)} %constant_dynamic-update-slice_fusion), channel_id=1, source_target_pairs={{0,192},{4,196},{8,200},{12,204},{16,208},{20,212},{24,216},{28,22... | collective-permute-start | bytes 393224 | tf_op jit(solution)/shard_map/ppermute | solution.py:368
  47.0 22.4 %collective-permute-start.23 = (bf16[256,256]{1,0:T(8,128)(2,1)S(1)}, bf16[256,256]{1,0:T(8,128)(2,1)S(1)}, u32[]{:S(2)}, u32[]{:S(2)}) collective-permute-start(bf16[256,256]{1,0:T(8,128)(2,1)S(1)} %collective-permute-done.22.kv0), channel_id=1, source_target_pairs={{0,16},{4,20},{8,24},{12,28},{16,32},{20,36},{24,40},{28,44},{32,4... | collective-permute-start | bytes 393224 | tf_op jit(solution)/shard_map/ppermute | solution.py:364
  49.7 19.8 %collective-permute-start.24 = (bf16[256,256]{1,0:T(8,128)(2,1)S(1)}, bf16[256,256]{1,0:T(8,128)(2,1)S(1)}, u32[]{:S(2)}, u32[]{:S(2)}) collective-permute-start(bf16[256,256]{1,0:T(8,128)(2,1)S(1)} %collective-permute-done.22.kv0), channel_id=1, source_target_pairs={{0,32},{4,36},{8,40},{12,44},{16,48},{20,52},{24,56},{28,60},{32,0... | collective-permute-start | bytes 393224 | tf_op jit(solution)/shard_map/ppermute | solution.py:364
  50.4 21.0 %collective-permute-start.25 = (bf16[256,256]{1,0:T(8,128)(2,1)S(1)}, bf16[256,256]{1,0:T(8,128)(2,1)S(1)}, u32[]{:S(2)}, u32[]{:S(2)}) collective-permute-start(bf16[256,256]{1,0:T(8,128)(2,1)S(1)} %collective-permute-done.22.kv0), channel_id=1, source_target_pairs={{0,48},{4,52},{8,56},{12,60},{16,0},{20,4},{24,8},{28,12},{32,16},... | collective-permute-start | bytes 393224 | tf_op jit(solution)/shard_map/ppermute | solution.py:364
  52.7 4.3 %collective-permute-start.5 = (bf16[272,128]{1,0:T(8,128)(2,1)S(1)}, bf16[272,128]{1,0:T(8,128)(2,1)S(1)}, u32[]{:S(2)}, u32[]{:S(2)}) collective-permute-start(bf16[272,128]{1,0:T(8,128)(2,1)S(1)} %get-tuple-element.49), channel_id=1, source_target_pairs={{0,48},{4,52},{8,56},{12,60},{16,0},{20,4},{24,8},{28,12},{32,16},... | collective-permute-start | bytes 208904 | tf_op jit(solution)/shard_map/ppermute | solution.py:364
  57.0 22.9 %collective-permute-start.27 = (bf16[256,256]{1,0:T(8,128)(2,1)S(1)}, bf16[256,256]{1,0:T(8,128)(2,1)S(1)}, u32[]{:S(2)}, u32[]{:S(2)}) collective-permute-start(bf16[256,256]{1,0:T(8,128)(2,1)S(1)} %collective-permute-done.26.kv0), channel_id=1, source_target_pairs={{0,16},{4,20},{8,24},{12,28},{16,32},{20,36},{24,40},{28,44},{32,4... | collective-permute-start | bytes 393224 | tf_op jit(solution)/shard_map/ppermute | solution.py:364
  60.4 19.8 %collective-permute-start.28 = (bf16[256,256]{1,0:T(8,128)(2,1)S(1)}, bf16[256,256]{1,0:T(8,128)(2,1)S(1)}, u32[]{:S(2)}, u32[]{:S(2)}) collective-permute-start(bf16[256,256]{1,0:T(8,128)(2,1)S(1)} %collective-permute-done.26.kv0), channel_id=1, source_target_pairs={{0,32},{4,36},{8,40},{12,44},{16,48},{20,52},{24,56},{28,60},{32,0... | collective-permute-start | bytes 393224 | tf_op jit(solution)/shard_map/ppermute | solution.py:364
  69.4 13.3 %collective-permute-start.29 = (bf16[256,256]{1,0:T(8,128)(2,1)S(1)}, bf16[256,256]{1,0:T(8,128)(2,1)S(1)}, u32[]{:S(2)}, u32[]{:S(2)}) collective-permute-start(bf16[256,256]{1,0:T(8,128)(2,1)S(1)} %collective-permute-done.26.kv0), channel_id=1, source_target_pairs={{0,48},{4,52},{8,56},{12,60},{16,0},{20,4},{24,8},{28,12},{32,16},... | collective-permute-start | bytes 393224 | tf_op jit(solution)/shard_map/ppermute | solution.py:364
  69.4 27.4 %collective-permute-start.31 = (bf16[256,256]{1,0:T(8,128)(2,1)S(1)}, bf16[256,256]{1,0:T(8,128)(2,1)S(1)}, u32[]{:S(2)}, u32[]{:S(2)}) collective-permute-start(bf16[256,256]{1,0:T(8,128)(2,1)S(1)} %collective-permute-done.30.kv0), channel_id=1, source_target_pairs={{0,16},{4,20},{8,24},{12,28},{16,32},{20,36},{24,40},{28,44},{32,4... | collective-permute-start | bytes 393224 | tf_op jit(solution)/shard_map/ppermute | solution.py:364
  71.5 12.5 %collective-permute-start.6 = (bf16[272,128]{1,0:T(8,128)(2,1)S(1)}, bf16[272,128]{1,0:T(8,128)(2,1)S(1)}, u32[]{:S(2)}, u32[]{:S(2)}) collective-permute-start(bf16[272,128]{1,0:T(8,128)(2,1)S(1)} %shard_map.115), channel_id=1, source_target_pairs={{0,64},{4,68},{8,72},{12,76},{16,80},{20,84},{24,88},{28,92},{32,9... | collective-permute-start | bytes 208904 | tf_op jit(solution)/shard_map/ppermute | solution.py:368
  79.9 18.2 %collective-permute-start.32 = (bf16[256,256]{1,0:T(8,128)(2,1)S(1)}, bf16[256,256]{1,0:T(8,128)(2,1)S(1)}, u32[]{:S(2)}, u32[]{:S(2)}) collective-permute-start(bf16[256,256]{1,0:T(8,128)(2,1)S(1)} %collective-permute-done.30.kv0), channel_id=1, source_target_pairs={{0,32},{4,36},{8,40},{12,44},{16,48},{20,52},{24,56},{28,60},{32,0... | collective-permute-start | bytes 393224 | tf_op jit(solution)/shard_map/ppermute | solution.py:364
  80.1 18.0 %collective-permute-start.33 = (bf16[256,256]{1,0:T(8,128)(2,1)S(1)}, bf16[256,256]{1,0:T(8,128)(2,1)S(1)}, u32[]{:S(2)}, u32[]{:S(2)}) collective-permute-start(bf16[256,256]{1,0:T(8,128)(2,1)S(1)} %collective-permute-done.30.kv0), channel_id=1, source_target_pairs={{0,48},{4,52},{8,56},{12,60},{16,0},{20,4},{24,8},{28,12},{32,16},... | collective-permute-start | bytes 393224 | tf_op jit(solution)/shard_map/ppermute | solution.py:364
  82.7 9.7 %collective-permute-start.7 = (bf16[272,128]{1,0:T(8,128)(2,1)S(1)}, bf16[272,128]{1,0:T(8,128)(2,1)S(1)}, u32[]{:S(2)}, u32[]{:S(2)}) collective-permute-start(bf16[272,128]{1,0:T(8,128)(2,1)S(1)} %shard_map.115), channel_id=1, source_target_pairs={{0,128},{4,132},{8,136},{12,140},{16,144},{20,148},{24,152},{28,15... | collective-permute-start | bytes 208904 | tf_op jit(solution)/shard_map/ppermute | solution.py:368
  84.0 9.2 %collective-permute-start.8 = (bf16[272,128]{1,0:T(8,128)(2,1)S(1)}, bf16[272,128]{1,0:T(8,128)(2,1)S(1)}, u32[]{:S(2)}, u32[]{:S(2)}) collective-permute-start(bf16[272,128]{1,0:T(8,128)(2,1)S(1)} %shard_map.115), channel_id=1, source_target_pairs={{0,192},{4,196},{8,200},{12,204},{16,208},{20,212},{24,216},{28,22... | collective-permute-start | bytes 208904 | tf_op jit(solution)/shard_map/ppermute | solution.py:368
  93.9 16.5 %collective-permute-start.9 = (bf16[256,128]{1,0:T(8,128)(2,1)S(1)}, bf16[256,128]{1,0:T(8,128)(2,1)S(1)}, u32[]{:S(2)}, u32[]{:S(2)}) collective-permute-start(bf16[256,128]{1,0:T(8,128)(2,1)S(1)} %get-tuple-element.51), channel_id=1, source_target_pairs={{0,16},{4,20},{8,24},{12,28},{16,32},{20,36},{24,40},{28,44},{32,4... | collective-permute-start | bytes 196616 | tf_op jit(solution)/shard_map/ppermute | solution.py:364
  94.0 16.7 %collective-permute-start.10 = (bf16[256,128]{1,0:T(8,128)(2,1)S(1)}, bf16[256,128]{1,0:T(8,128)(2,1)S(1)}, u32[]{:S(2)}, u32[]{:S(2)}) collective-permute-start(bf16[256,128]{1,0:T(8,128)(2,1)S(1)} %get-tuple-element.52), channel_id=1, source_target_pairs={{0,32},{4,36},{8,40},{12,44},{16,48},{20,52},{24,56},{28,60},{32,0... | collective-permute-start | bytes 196616 | tf_op jit(solution)/shard_map/ppermute | solution.py:364
  96.8 13.8 %collective-permute-start.11 = (bf16[256,128]{1,0:T(8,128)(2,1)S(1)}, bf16[256,128]{1,0:T(8,128)(2,1)S(1)}, u32[]{:S(2)}, u32[]{:S(2)}) collective-permute-start(bf16[256,128]{1,0:T(8,128)(2,1)S(1)} %get-tuple-element.53), channel_id=1, source_target_pairs={{0,48},{4,52},{8,56},{12,60},{16,0},{20,4},{24,8},{28,12},{32,16},... | collective-permute-start | bytes 196616 | tf_op jit(solution)/shard_map/ppermute | solution.py:364
  107.0 11.3 %collective-permute-start.34 = (bf16[128,640]{1,0:T(8,128)(2,1)S(1)}, bf16[128,640]{1,0:T(8,128)(2,1)S(1)}, u32[]{:S(2)}, u32[]{:S(2)}) collective-permute-start(bf16[128,640]{1,0:T(8,128)(2,1)S(1)} %get-tuple-element.79), channel_id=1, source_target_pairs={{0,12},{4,0},{8,4},{12,8},{16,28},{20,16},{24,20},{28,24},{32,44},... | collective-permute-start | bytes 491528 | tf_op jit(solution)/shard_map/ppermute | solution.py:360
  109.1 10.6 %collective-permute-start.35 = (bf16[128,640]{1,0:T(8,128)(2,1)S(1)}, bf16[128,640]{1,0:T(8,128)(2,1)S(1)}, u32[]{:S(2)}, u32[]{:S(2)}) collective-permute-start(bf16[128,640]{1,0:T(8,128)(2,1)S(1)} %get-tuple-element.80), channel_id=1, source_target_pairs={{0,8},{4,12},{8,0},{12,4},{16,24},{20,28},{24,16},{28,20},{32,40},... | collective-permute-start | bytes 491528 | tf_op jit(solution)/shard_map/ppermute | solution.py:360
  110.4 9.3 %collective-permute-start.36 = (bf16[128,640]{1,0:T(8,128)(2,1)S(1)}, bf16[128,640]{1,0:T(8,128)(2,1)S(1)}, u32[]{:S(2)}, u32[]{:S(2)}) collective-permute-start(bf16[128,640]{1,0:T(8,128)(2,1)S(1)} %get-tuple-element.81), channel_id=1, source_target_pairs={{0,4},{4,8},{8,12},{12,0},{16,20},{20,24},{24,28},{28,16},{32,36},... | collective-permute-start | bytes 491528 | tf_op jit(solution)/shard_map/ppermute | solution.py:360
  114.4 10.3 %copy-start.2 = (bf16[128,2048]{1,0:T(8,128)(2,1)S(1)}, bf16[128,2048]{1,0:T(8,128)(2,1)}, u32[]{:S(2)}) copy-start(bf16[128,2048]{1,0:T(8,128)(2,1)} %gate.1) | copy-start | bytes 1572868
  114.4 7.4 %collective-permute-start.12 = (bf16[128,512]{1,0:T(8,128)(2,1)S(1)}, bf16[128,512]{1,0:T(8,128)(2,1)S(1)}, u32[]{:S(2)}, u32[]{:S(2)}) collective-permute-start(bf16[128,512]{1,0:T(8,128)(2,1)S(1)} %get-tuple-element.55), channel_id=1, source_target_pairs={{0,4},{4,8},{8,12},{12,0},{16,20},{20,24},{24,28},{28,16},{32,36},... | collective-permute-start | bytes 393224 | tf_op jit(solution)/shard_map/ppermute | solution.py:360
  117.0 6.6 %collective-permute-start.13 = (bf16[128,512]{1,0:T(8,128)(2,1)S(1)}, bf16[128,512]{1,0:T(8,128)(2,1)S(1)}, u32[]{:S(2)}, u32[]{:S(2)}) collective-permute-start(bf16[128,512]{1,0:T(8,128)(2,1)S(1)} %get-tuple-element.56), channel_id=1, source_target_pairs={{0,8},{4,12},{8,0},{12,4},{16,24},{20,28},{24,16},{28,20},{32,40},... | collective-permute-start | bytes 393224 | tf_op jit(solution)/shard_map/ppermute | solution.py:360
  118.3 6.4 %collective-permute-start.14 = (bf16[128,512]{1,0:T(8,128)(2,1)S(1)}, bf16[128,512]{1,0:T(8,128)(2,1)S(1)}, u32[]{:S(2)}, u32[]{:S(2)}) collective-permute-start(bf16[128,512]{1,0:T(8,128)(2,1)S(1)} %get-tuple-element.57), channel_id=1, source_target_pairs={{0,12},{4,0},{8,4},{12,8},{16,28},{20,16},{24,20},{28,24},{32,44},... | collective-permute-start | bytes 393224 | tf_op jit(solution)/shard_map/ppermute | solution.py:360
  119.7 5.0 %copy-start.8 = (f32[2048]{0:T(1024)S(1)}, f32[2048]{0:T(1024)}, u32[]{:S(2)}) copy-start(f32[2048]{0:T(1024)} %param.16) | copy-start | bytes 24580
